TPU v7x, 32 devices: a whole 2x2x4 slice. The times are simulated.
32 devices in a mesh: front: 2 (over x), row: 4 (over z), col: 4 (over y, core).
Axes of the slice: x: 2, y: 2, z: 4, core: 2. Of those that a mesh axis runs over, the one named last changes fastest.
Arguments:
- child_blocks: float32 [2, 4, 4, 2, 8, 128, 128], P('front', 'row', 'col'), may hold values from -0.15232572 to 0.15232572
- child_map: int32 [2, 4, 4, 2, 8], P('front', 'row', 'col'), may hold values from 0 to 63
- stiff_diag: float32 [2, 4096], P('front'), may hold values from 2.5 to 4
- pivot_blocks: int32 [2], P('front'), may hold values from 1 to 4, as said below
Outputs:
- factored: float32 [2, 4, 8, 128, 4, 8, 128], P('front', 'row', None, None, 'col')
Inputs may be any that keep to these rules, and one draw needn't show every extreme that they name: `pivot_blocks`: exactly one front has 4; every other front has fewer.
All inputs are finite; a program needn't handle non-finite values.
Results may differ from a plain program's by a relative error of at most 0.0003.
Values sent between devices are 32-bit elements; how exact they have to be, the bound alone decides.
A program may use at most 128 MiB of HBM per device.

v0:
```python
import functools

import jax
import jax.numpy as jnp
from jax import lax
from jax.experimental import pallas as pl
from jax.experimental.pallas import tpu as pltpu
from jax.sharding import PartitionSpec as P

NP = 4
GROUP = 4
NT = (((1,), (1,)), ((), ()))
TN = (((0,), (0,)), ((), ()))
NN = (((1,), (0,)), ((), ()))
F32 = jnp.float32
BF16 = jnp.bfloat16
VMEM_BYTES = 44 * 1024 * 1024


def exact_dot(a, b, dims):
    return lax.dot_general(
        a, b, dims, precision=lax.Precision.HIGHEST, preferred_element_type=F32
    )


def split(x):
    high = x.astype(BF16)
    return high, (x - high.astype(F32)).astype(BF16)


def split_dot(a, b, dims):
    dot = functools.partial(lax.dot_general, dimension_numbers=dims, preferred_element_type=F32)
    return dot(a[0], b[0]) + (dot(a[0], b[1]) + dot(a[1], b[0]))


def panel_kernel(slots, across, targets, blocks, out):
    out[...] = jnp.zeros_like(out)

    def body(s, carry):
        t = targets[s]

        @pl.when(lax.rem(t, across) == 0)
        def _():
            i = lax.div(t, across)
            out[i] = out[i] + blocks[s]

        return carry

    lax.fori_loop(0, slots, body, 0)


def invert_diagonal(block, bs):
    tiles = bs // 8
    sub = lax.broadcasted_iota(jnp.int32, (8, bs), 0)
    lane = lax.broadcasted_iota(jnp.int32, (8, bs), 1)
    m = [block[8 * i : 8 * i + 8, :] for i in range(tiles)]
    w = [(lane == sub + 8 * i).astype(F32) for i in range(tiles)]
    for k in range(0, bs, GROUP):
        top = k // 8
        cols = [
            {
                i: jnp.broadcast_to(m[i][:, k + t : k + t + 1], (8, bs))
                for i in range(top, tiles)
            }
            for t in range(GROUP)
        ]
        for t in range(GROUP):
            kk = k % 8 + t
            inv = 1.0 / cols[t][top][kk : kk + 1, :]
            q = m[top][kk : kk + 1, :] * inv
            wq = w[top][kk : kk + 1, :] * inv
            rest = {s: cols[s][top][kk : kk + 1, :] * inv for s in range(t + 1, GROUP)}
            for i in range(top, tiles):
                c = cols[t][i]
                if i == top:
                    if kk == 7:
                        continue
                    c = jnp.where(sub > kk, c, 0.0)
                m[i] = m[i] - c * q
                w[i] = w[i] - c * wq
                for s in rest:
                    cols[s][i] = cols[s][i] - c * rest[s]
    out = []
    for i in range(tiles):
        d = jnp.sum(jnp.where(lane == sub + 8 * i, m[i], 0.0), axis=1, keepdims=True)
        out.append(w[i] * lax.rsqrt(d))
    return jnp.concatenate(out, axis=0)


def factor_kernel(bs, scal, lead, stiff, inverse, full, work):
    n = NP * bs
    pivot = scal[2]
    row = lax.broadcasted_iota(jnp.int32, (bs, bs), 0)
    col = lax.broadcasted_iota(jnp.int32, (bs, bs), 1)
    eye = row == col
    for i in range(NP):
        for j in range(i + 1):
            block = lead[i * NP + j]
            if i == j:
                block = jnp.where(row >= col, block, block.T)
                block = block + jnp.where(eye, stiff[i : i + 1, :], 0.0)
            full[i * bs : (i + 1) * bs, j * bs : (j + 1) * bs] = block
            if i != j:
                full[j * bs : (j + 1) * bs, i * bs : (i + 1) * bs] = block.T
    for i in range(NP):
        for j in range(NP):
            ok = jnp.logical_and(i < pivot, j < pivot)
            rest = eye.astype(F32) if i == j else jnp.zeros((bs, bs), F32)
            work[i * bs : (i + 1) * bs, j * bs : (j + 1) * bs] = jnp.where(
                ok, full[i * bs : (i + 1) * bs, j * bs : (j + 1) * bs], rest
            )
            work[i * bs : (i + 1) * bs, n + j * bs : n + (j + 1) * bs] = (
                eye.astype(F32) if i == j else jnp.zeros((bs, bs), F32)
            )

    for b in range(NP):
        lo, hi = b * bs, (b + 1) * bs
        w = invert_diagonal(work[lo:hi, lo:hi], bs)
        done = exact_dot(w, work[lo:hi, lo : n + hi], NN)
        inverse[lo:hi, :] = jnp.where(b < pivot, jnp.concatenate(
            [done[:, n - lo :]] + ([jnp.zeros((bs, n - hi), F32)] if hi < n else []), axis=1
        ), 0.0)
        if hi < n:
            work[hi:, hi : n + hi] = work[hi:, hi : n + hi] - exact_dot(
                done[:, bs : n - lo], done[:, bs:], TN
            )


def update_kernel(
    slots, across, rows_n, cols_n, bs, scal, targets, blocks, row_part, col_part, full, inverse,
    stiff, out, inv_hi, inv_lo, col_hi, col_lo, total,
):
    i = pl.program_id(0)
    down = pl.num_programs(0)
    r, c, pivot = scal[0], scal[1], scal[2]

    def solved(part, k, place):
        def first():
            return full[pl.ds(pl.multiple_of(place * bs, bs), bs), :]

        a = jnp.concatenate([part[j, jnp.maximum(k - 1, 0)] for j in range(NP)], axis=1)
        a = jnp.where(k == 0, first(), a)
        return split_dot(split(a), (inv_hi[...], inv_lo[...]), NT)

    @pl.when(i == 0)
    def _():
        high, low = split(inverse[...])
        inv_hi[...] = high
        inv_lo[...] = low

    high, low = split(solved(col_part, i, c))
    at = pl.ds(pl.multiple_of(i * bs, bs), bs)
    col_hi[at, :] = high
    col_lo[at, :] = low
    x = solved(row_part, i, r)
    mine = split(x)
    total[...] = jnp.zeros_like(total)

    def body(s, carry):
        t = targets[s]

        @pl.when(lax.div(t, across) == i)
        def _():
            j = lax.rem(t, across)
            total[j] = total[j] + blocks[s]

        return carry

    lax.fori_loop(0, slots, body, 0)
    place = r + rows_n * i
    row = lax.broadcasted_iota(jnp.int32, (bs, bs), 0)
    col = lax.broadcasted_iota(jnp.int32, (bs, bs), 1)
    stiff_row = stiff[pl.ds(place, 1), :]

    for j in range(across):
        across_place = c + cols_n * j

        @pl.when(place > across_place)
        def _():
            at_j = slice(j * bs, (j + 1) * bs)
            v = total[j] - split_dot(mine, (col_hi[at_j, :], col_lo[at_j, :]), NT)
            total[j] = v

        @pl.when(place == across_place)
        def _():
            at_j = slice(j * bs, (j + 1) * bs)
            v = total[j] - split_dot(mine, (col_hi[at_j, :], col_lo[at_j, :]), NT)
            v = v + jnp.where(row == col, stiff_row, 0.0)
            total[j] = jnp.where(row >= col, v, 0.0)

        if j == 0:
            for b in range(NP):

                @pl.when((c == b) & (b < pivot))
                def _():
                    mask = (place > b) | ((place == b) & (row >= col))
                    total[0] = jnp.where(mask, x[:, b * bs : (b + 1) * bs], 0.0)

        out[0, pl.ds(j, bs, stride=across), :] = total[j]


def on_device(child_blocks, child_map, stiff_diag, pivot_blocks):
    frames, slot_count, bs = child_blocks.shape[3:6]
    rows_n, cols_n = lax.axis_size("row"), lax.axis_size("col")
    order = stiff_diag.shape[1]
    down, across = order // (bs * rows_n), order // (bs * cols_n)
    slots = frames * slot_count
    r, c = lax.axis_index("row"), lax.axis_index("col")
    scal = jnp.stack([r, c, pivot_blocks[0]]).astype(jnp.int32)
    targets = child_map.reshape(slots)
    stiff = stiff_diag.reshape(order // bs, bs)
    outgoing = child_blocks.reshape(frames, slot_count, bs, bs)
    incoming = lax.all_to_all(outgoing, "front", split_axis=0, concat_axis=0, tiled=True)
    blocks = incoming.reshape(slots, bs, bs)
    smem = pl.BlockSpec(memory_space=pltpu.SMEM)
    vmem = pl.BlockSpec(memory_space=pltpu.VMEM)
    params = pltpu.CompilerParams(vmem_limit_bytes=VMEM_BYTES)
    panel = pl.pallas_call(
        functools.partial(panel_kernel, slots, across),
        out_shape=jax.ShapeDtypeStruct((down, bs, bs), F32),
        in_specs=[smem, vmem],
        out_specs=vmem,
        compiler_params=params,
    )(targets, blocks)
    lead = lax.all_gather(panel[0], ("row", "col"), axis=0, tiled=False)
    piece = panel[1:]
    turned = lax.ppermute(
        piece,
        ("row", "col"),
        [(a * cols_n + b, b * cols_n + a) for a in range(rows_n) for b in range(cols_n)],
    )
    row_part = lax.all_gather(piece, "col", axis=0, tiled=False)
    col_part = lax.all_gather(turned, "row", axis=0, tiled=False)
    n = NP * bs
    inverse, full = pl.pallas_call(
        functools.partial(factor_kernel, bs),
        out_shape=[jax.ShapeDtypeStruct((n, n), F32)] * 2,
        in_specs=[smem, vmem, vmem],
        out_specs=[vmem, vmem],
        scratch_shapes=[pltpu.VMEM((n, 2 * n), F32)],
        compiler_params=params,
        cost_estimate=pl.CostEstimate(
            flops=20_000_000_000, bytes_accessed=4 * 1024 * 1024, transcendentals=0
        ),
    )(scal, lead, stiff[:NP])

    def whole(shape):
        return pl.BlockSpec(shape, lambda i: (0,) * len(shape))

    result = pl.pallas_call(
        functools.partial(update_kernel, slots, across, rows_n, cols_n, bs),
        grid=(down,),
        out_shape=jax.ShapeDtypeStruct((down, bs * across, bs), F32),
        in_specs=[
            smem,
            smem,
            whole(blocks.shape),
            whole(row_part.shape),
            whole(col_part.shape),
            whole((n, n)),
            whole((n, n)),
            whole(stiff.shape),
        ],
        out_specs=pl.BlockSpec((1, bs * across, bs), lambda i: (i, 0, 0)),
        scratch_shapes=[
            pltpu.VMEM((n, n), BF16),
            pltpu.VMEM((n, n), BF16),
            pltpu.VMEM((across * bs, n), BF16),
            pltpu.VMEM((across * bs, n), BF16),
            pltpu.VMEM((across, bs, bs), F32),
        ],
        compiler_params=params,
    )(scal, targets, blocks, row_part, col_part, full, inverse, stiff)
    return result.reshape(1, 1, down, bs, 1, across, bs)


def solution(mesh):
    placed = (
        P("front", "row", "col", None, None, None, None),
        P("front", "row", "col", None, None),
        P("front", None),
        P("front"),
    )
    return jax.shard_map(
        on_device,
        mesh=mesh,
        in_specs=placed,
        out_specs=P("front", "row", None, None, "col", None, None),
        check_vma=False,
    )
```

profile of v0, /device:TPU:17, one launch (start us, length us, event | category | flops | bytes accessed | tf_op | source)
XLA Modules:
  0.0 166.0 jit_solution(4157983168166307787)
XLA Ops:
  6.5 0.0 copy-start.5
  6.5 3.7 %all-to-all-start = ((f32[2,8,128,128]{3,2,1,0:T(8,128)}), f32[2,8,128,128]{3,2,1,0:T(8,128)S(1)}, u32[]{:S(2)}, u32[]{:S(2)}) async-start(f32[2,8,128,128]{3,2,1,0:T(8,128)} %bitcast.17), calls=%async_computation | async-start | bytes 2097152 | tf_op jit(solution)/shard_map/all_to_all | solution.py:213
  10.3 0.0 copy-start.2
  10.3 0.0 all-gather.6.cloned.1.call-start
  10.3 0.0 copy-done.5
  10.3 0.1 reshape.16.targets
  10.4 12.8 %all-to-all-done = f32[2,8,128,128]{3,2,1,0:T(8,128)S(1)} async-done(((f32[2,8,128,128]{3,2,1,0:T(8,128)}), f32[2,8,128,128]{3,2,1,0:T(8,128)S(1)}, u32[]{:S(2)}, u32[]{:S(2)}) %all-to-all-start) | async-done | bytes 1048608 | tf_op jit(solution)/shard_map/all_to_all | solution.py:213
  23.2 0.9 shard_map.46
  24.1 0.6 slice.17
  24.7 0.0 all-gather.6.cloned.1.call-update
  24.8 0.0 all-gather.8.cloned.1.call-start
  24.8 0.8 slice.16
  25.6 0.0 all-gather.8.cloned.1.call-update
  25.6 0.0 all-gather.10.cloned.1.call-start
  25.7 4.5 %collective-permute-start = (f32[7,128,128]{2,1,0:T(8,128)}, f32[7,128,128]{2,1,0:T(8,128)S(1)}, u32[]{:S(2)}, u32[]{:S(2)}) collective-permute-start(f32[7,128,128]{2,1,0:T(8,128)} %slice.16), channel_id=1, source_target_pairs={{0,0},{1,4},{2,8},{3,12},{4,1},{5,5},{6,9},{7,13},{8,2},{9,6},{10,... | collective-permute-start | bytes 1376264 | tf_op jit(solution)/shard_map/ppermute | solution.py:227
  30.2 22.9 %collective-permute-done = f32[7,128,128]{2,1,0:T(8,128)S(1)} collective-permute-done((f32[7,128,128]{2,1,0:T(8,128)}, f32[7,128,128]{2,1,0:T(8,128)S(1)}, u32[]{:S(2)}, u32[]{:S(2)}) %collective-permute-start) | collective-permute-done | bytes 458784 | tf_op jit(solution)/shard_map/ppermute | solution.py:227
  53.1 0.0 copy-start.4
  53.1 0.8 copy-done.4
  53.9 0.0 all-gather.10.cloned.1.call-update
  54.5 0.0 copy-done.2
  54.6 0.1 pad_add_fusion.scal
  54.6 12.8 %all-gather.6.cloned.1.call-done.lead = f32[16,128,128]{2,1,0:T(8,128)} async-done(((f32[1,128,128]{2,1,0:T(8,128)}), f32[16,128,128]{2,1,0:T(8,128)}) %all-gather.6.cloned.1.call-update) | async-done | bytes 1048592 | tf_op jit(solution)/shard_map/all_gather | solution.py:225
  67.4 0.0 copy-start.3
  67.4 1.2 copy-done.3
  68.7 22.0 %shard_map.47 = (f32[512,512]{1,0:T(8,128)S(1)}, f32[512,512]{1,0:T(8,128)S(1)}) custom-call(s32[3]{0:T(128)S(1)} %pad_add_fusion.scal, f32[16,128,128]{2,1,0:T(8,128)S(1)} %copy-done.3, f32[4,128]{1,0:T(4,128)S(1)} %bitcast.16), custom_call_target="tpu_custom_call" | custom-call | flops 20000000000 | bytes 4194304 | tf_op jit(solution)/shard_map/pallas_call | solution.py:235
  90.7 0.1 all-gather.8.cloned.1.call-done
  90.8 41.4 %all-gather.10.cloned.1.call-done = f32[28,128,128]{2,1,0:T(8,128)} async-done(((f32[7,128,128]{2,1,0:T(8,128)}), f32[28,128,128]{2,1,0:T(8,128)}) %all-gather.10.cloned.1.call-update) | async-done | bytes 1835024 | tf_op jit(solution)/shard_map/all_gather | solution.py:233
  132.2 0.0 copy-start
  132.2 1.5 copy-done
  133.7 0.0 copy-start.1
  133.7 1.5 copy-done.1
  135.2 24.2 %shard_map.48 = f32[8,1024,128]{2,1,0:T(8,128)} custom-call(s32[3]{0:T(128)S(1)} %pad_add_fusion.scal, s32[16]{0:T(128)S(1)} %reshape.16.targets, f32[16,128,128]{2,1,0:T(8,128)S(1)} %bitcast.12, f32[4,7,128,128]{3,2,1,0:T(8,128)S(1)} %bitcast.13, f32[4,7,128,128]{3,2,1,0:T(8,128)S(1)} %bitcast.14, f32[512,512]{1,0:T(8,128)S(1)} %get-tuple-element.7.full, ...), custom_call_target="tpu_custom_call" | custom-call | tf_op jit(solution)/shard_map/pallas_call | solution.py:250
  (1 shorter events, 0.0 us)
Async XLA Ops:
  6.5 3.8 %copy-start.5 = (s32[1,1,1,2,8]{4,3,2,1,0:T(2,128)S(1)}, s32[1,1,1,2,8]{4,3,2,1,0:T(2,128)}, u32[]{:S(2)}) copy-start(s32[1,1,1,2,8]{4,3,2,1,0:T(2,128)} %param.5) | copy-start | bytes 196
  6.5 16.7 %all-to-all-start = ((f32[2,8,128,128]{3,2,1,0:T(8,128)}), f32[2,8,128,128]{3,2,1,0:T(8,128)S(1)}, u32[]{:S(2)}, u32[]{:S(2)}) async-start(f32[2,8,128,128]{3,2,1,0:T(8,128)} %bitcast.17), calls=%async_computation | async-start | bytes 2097152 | tf_op jit(solution)/shard_map/all_to_all | solution.py:213
  10.3 44.3 %copy-start.2 = (f32[1,4096]{1,0:T(1,128)S(1)}, f32[1,4096]{1,0:T(1,128)}, u32[]{:S(2)}) copy-start(f32[1,4096]{1,0:T(1,128)} %param.6) | copy-start | bytes 49156
  10.3 57.2 %all-gather.6.cloned.1.call-start = ((), (), s32[]{:S(2)}) async-start(), calls=%async_computation.1 | async-start | bytes 1114112 | tf_op jit(solution)/shard_map/all_gather | solution.py:225
  24.8 66.0 %all-gather.8.cloned.1.call-start = ((), (), s32[]{:S(2)}) async-start(), calls=%async_computation.2 | async-start | bytes 2293760 | tf_op jit(solution)/shard_map/all_gather | solution.py:232
  25.6 106.6 %all-gather.10.cloned.1.call-start = ((), (), s32[]{:S(2)}) async-start(), calls=%async_computation.3 | async-start | bytes 2293760 | tf_op jit(solution)/shard_map/all_gather | solution.py:233
  25.7 27.4 %collective-permute-start = (f32[7,128,128]{2,1,0:T(8,128)}, f32[7,128,128]{2,1,0:T(8,128)S(1)}, u32[]{:S(2)}, u32[]{:S(2)}) collective-permute-start(f32[7,128,128]{2,1,0:T(8,128)} %slice.16), channel_id=1, source_target_pairs={{0,0},{1,4},{2,8},{3,12},{4,1},{5,5},{6,9},{7,13},{8,2},{9,6},{10,... | collective-permute-start | bytes 1376264 | tf_op jit(solution)/shard_map/ppermute | solution.py:227
  53.1 0.8 copy-start.4
  67.4 1.2 copy-start.3
  132.2 1.5 copy-start
  133.7 1.5 copy-start.1
Sparse Core Ops, SparseCore 0:
  24.9 42.5 all-gather.5
  69.0 21.7 all-gather.7
  92.4 39.7 all-gather.9
where the time goes:
time: 169 us; the launch traced here: 166 us
  waiting for transfers between devices  90.1 us (53%)
  Pallas kernels  47.1 us (28%)
  between operations  13.8 us (8%)
  starting transfers between devices  8.33 us (5%)
  local copies, waits for them, and re-layouts  6.51 us (4%)
    all_gather x1, waiting for transfers between devices, on_device(): col_part = lax.all_gather(turned, 'row', axis=0, tiled=False)  41.4 us
    pallas_call x1, Pallas kernels, on_device(): pl.pallas_call(functools.partial(update_kernel, slots, across, rows_n, co...  24.2 us
    ppermute x1, waiting for transfers between devices, on_device(): lax.ppermute(piece, ('row', 'col'), [(a * cols_n + b, b * cols_n + a) for...  22.9 us
    pallas_call x1, Pallas kernels, on_device(): pl.pallas_call(functools.partial(factor_kernel, bs), out_shape=[jax.Shape...  22 us
    all_to_all x1, waiting for transfers between devices, on_device(): lax.all_to_all(outgoing, 'front', split_axis=0, concat_axis=0, tiled=True)  12.8 us
    all_gather x1, waiting for transfers between devices, on_device(): lead = lax.all_gather(panel[0], ('row', 'col'), axis=0, tiled=False)  12.8 us
    unnamed x12, local copies, waits for them, and re-layouts  5 us
    ppermute x1, starting transfers between devices, on_device(): lax.ppermute(piece, ('row', 'col'), [(a * cols_n + b, b * cols_n + a) for...  4.49 us
  transfers between devices with their start and end apart: 5, of which 5 were waited for; matrix products, arithmetic and copies ran while one was open for 1% of the time, Pallas kernels for 13%

commit v1 on v0

--- a/solution.py
+++ b/solution.py
@@ -134,11 +134,11 @@
     down = pl.num_programs(0)
     r, c, pivot = scal[0], scal[1], scal[2]
 
-    def solved(part, k, place):
+    def solved(part, k, place, owners):
         def first():
             return full[pl.ds(pl.multiple_of(place * bs, bs), bs), :]
 
-        a = jnp.concatenate([part[j, jnp.maximum(k - 1, 0)] for j in range(NP)], axis=1)
+        a = jnp.concatenate([part[owner, jnp.maximum(k - 1, 0)] for owner in owners], axis=1)
         a = jnp.where(k == 0, first(), a)
         return split_dot(split(a), (inv_hi[...], inv_lo[...]), NT)
 
@@ -148,11 +148,11 @@
         inv_hi[...] = high
         inv_lo[...] = low
 
-    high, low = split(solved(col_part, i, c))
+    high, low = split(solved(col_part, i, c, [lax.rem(r - j + rows_n, rows_n) for j in range(NP)]))
     at = pl.ds(pl.multiple_of(i * bs, bs), bs)
     col_hi[at, :] = high
     col_lo[at, :] = low
-    x = solved(row_part, i, r)
+    x = solved(row_part, i, r, range(NP))
     mine = split(x)
     total[...] = jnp.zeros_like(total)
 
@@ -224,13 +224,20 @@
     )(targets, blocks)
     lead = lax.all_gather(panel[0], ("row", "col"), axis=0, tiled=False)
     piece = panel[1:]
-    turned = lax.ppermute(
-        piece,
-        ("row", "col"),
-        [(a * cols_n + b, b * cols_n + a) for a in range(rows_n) for b in range(cols_n)],
-    )
+    turned = [
+        lax.ppermute(
+            piece,
+            ("row", "col"),
+            [
+                (a * cols_n + b, (b + k) % rows_n * cols_n + a)
+                for a in range(rows_n)
+                for b in range(cols_n)
+            ],
+        )
+        for k in range(NP)
+    ]
     row_part = lax.all_gather(piece, "col", axis=0, tiled=False)
-    col_part = lax.all_gather(turned, "row", axis=0, tiled=False)
+    col_part = jnp.stack(turned)
     n = NP * bs
     inverse, full = pl.pallas_call(
         functools.partial(factor_kernel, bs),

time: 169 us -> 142 us (0.84)
  waiting for transfers between devices: 90.1 us -> 57.7 us
  starting transfers between devices: 8.33 us -> 10.8 us
  local copies, waits for them, and re-layouts: 6.51 us -> 8.95 us
    all_gather x1 -> x0, waiting for transfers between devices: 41.4 us -> none  [on_device(): col_part = lax.all_gather(turned, 'row', axis=0, tiled=False)]
    ppermute x1 -> x4, waiting for transfers between devices: 22.9 us -> 42.1 us  [on_device(): lax.ppermute(piece, ('row', 'col'), [(a * cols_n + b, (b + k) % rows_n *...]
    all_gather x1, waiting for transfers between devices: 12.8 us -> 2.75 us  [on_device(): lead = lax.all_gather(panel[0], ('row', 'col'), axis=0, tiled=False)]
    ppermute x1 -> x4, starting transfers between devices: 4.49 us -> 7.05 us  [on_device(): lax.ppermute(piece, ('row', 'col'), [(a * cols_n + b, (b + k) % rows_n *...]
    unnamed x12 -> x18, local copies, waits for them, and re-layouts: 5 us -> 7.45 us
  transfers between devices with their start and end apart: 5 -> 7, of which waited for: 5 -> 5; matrix products, arithmetic and copies ran while one was open for 1% -> 2% of each run, Pallas kernels for 13% -> 16%
where the time goes in v1:
time: 142 us; the launch traced here: 140 us
  waiting for transfers between devices  57.7 us (41%)
  Pallas kernels  47.2 us (33%)
  between operations  14.1 us (10%)
  starting transfers between devices  10.8 us (8%)
  local copies, waits for them, and re-layouts  8.95 us (6%)
  other arithmetic  1.55 us (1%)
    ppermute x4, waiting for transfers between devices, on_device(): lax.ppermute(piece, ('row', 'col'), [(a * cols_n + b, (b + k) % rows_n *...  42.1 us
    pallas_call x1, Pallas kernels, on_device(): pl.pallas_call(functools.partial(update_kernel, slots, across, rows_n, co...  24.3 us
    pallas_call x1, Pallas kernels, on_device(): pl.pallas_call(functools.partial(factor_kernel, bs), out_shape=[jax.Shape...  22 us
    all_to_all x1, waiting for transfers between devices, on_device(): lax.all_to_all(outgoing, 'front', split_axis=0, concat_axis=0, tiled=True)  12.8 us
    unnamed x18, local copies, waits for them, and re-layouts  7.45 us
    ppermute x4, starting transfers between devices, on_device(): lax.ppermute(piece, ('row', 'col'), [(a * cols_n + b, (b + k) % rows_n *...  7.05 us
    all_to_all x1, starting transfers between devices, on_device(): lax.all_to_all(outgoing, 'front', split_axis=0, concat_axis=0, tiled=True)  3.71 us
  transfers between devices with their start and end apart: 7, of which 5 were waited for; matrix products, arithmetic and copies ran while one was open for 2% of the time, Pallas kernels for 16%

profile of v1, /device:TPU:17, one launch (start us, length us, event | category | flops | bytes accessed | tf_op | source)
XLA Modules:
  0.0 140.4 jit_solution(1790974248151333016)
XLA Ops:
  6.5 0.0 copy-start.8
  6.5 3.7 %all-to-all-start = ((f32[2,8,128,128]{3,2,1,0:T(8,128)}), f32[2,8,128,128]{3,2,1,0:T(8,128)S(1)}, u32[]{:S(2)}, u32[]{:S(2)}) async-start(f32[2,8,128,128]{3,2,1,0:T(8,128)} %bitcast.19), calls=%async_computation | async-start | bytes 2097152 | tf_op jit(solution)/shard_map/all_to_all | solution.py:213
  10.3 0.0 copy-start.5
  10.3 0.0 all-gather.4.cloned.1.call-start
  10.3 0.0 copy-done.8
  10.3 0.1 reshape.16.targets
  10.4 12.8 %all-to-all-done = f32[2,8,128,128]{3,2,1,0:T(8,128)S(1)} async-done(((f32[2,8,128,128]{3,2,1,0:T(8,128)}), f32[2,8,128,128]{3,2,1,0:T(8,128)S(1)}, u32[]{:S(2)}, u32[]{:S(2)}) %all-to-all-start) | async-done | bytes 1048608 | tf_op jit(solution)/shard_map/all_to_all | solution.py:213
  23.2 0.8 shard_map.46
  24.1 0.6 slice.17
  24.7 0.0 all-gather.4.cloned.1.call-update
  24.7 0.0 all-gather.6.cloned.1.call-start
  24.8 0.8 slice.16
  25.6 0.0 all-gather.6.cloned.1.call-update
  25.6 2.5 %collective-permute-start.3 = (f32[7,128,128]{2,1,0:T(8,128)}, f32[7,128,128]{2,1,0:T(8,128)S(1)}, u32[]{:S(2)}, u32[]{:S(2)}) collective-permute-start(f32[7,128,128]{2,1,0:T(8,128)} %slice.16), channel_id=1, source_target_pairs={{0,12},{1,0},{2,4},{3,8},{4,13},{5,1},{6,5},{7,9},{8,14},{9,2},{10... | collective-permute-start | bytes 1376264 | tf_op jit(solution)/shard_map/ppermute | solution.py:228
  28.1 1.3 collective-permute-start.2
  29.4 0.8 collective-permute-start.1
  30.2 2.5 %collective-permute-start = (f32[7,128,128]{2,1,0:T(8,128)}, f32[7,128,128]{2,1,0:T(8,128)}, u32[]{:S(2)}, u32[]{:S(2)}) collective-permute-start(f32[7,128,128]{2,1,0:T(8,128)} %slice.16), channel_id=1, source_target_pairs={{0,0},{1,4},{2,8},{3,12},{4,1},{5,5},{6,9},{7,13},{8,2},{9,6},{10,... | collective-permute-start | bytes 1376264 | tf_op jit(solution)/shard_map/ppermute | solution.py:228
  33.3 0.0 copy-done.5
  33.3 0.1 pad_add_fusion.scal
  33.4 13.3 %collective-permute-done.3 = f32[7,128,128]{2,1,0:T(8,128)S(1)} collective-permute-done((f32[7,128,128]{2,1,0:T(8,128)}, f32[7,128,128]{2,1,0:T(8,128)S(1)}, u32[]{:S(2)}, u32[]{:S(2)}) %collective-permute-start.3) | collective-permute-done | bytes 458784 | tf_op jit(solution)/shard_map/ppermute | solution.py:228
  46.7 28.3 %collective-permute-done.2 = f32[7,128,128]{2,1,0:T(8,128)S(1)} collective-permute-done((f32[7,128,128]{2,1,0:T(8,128)}, f32[7,128,128]{2,1,0:T(8,128)S(1)}, u32[]{:S(2)}, u32[]{:S(2)}) %collective-permute-start.2) | collective-permute-done | bytes 458784 | tf_op jit(solution)/shard_map/ppermute | solution.py:228
  75.0 0.0 copy-start.7
  75.0 0.4 collective-permute-done.1
  75.5 0.0 collective-permute-done
  75.5 0.3 copy-done.7
  75.8 1.5 %pad_maximum_fusion.col_part = f32[4,7,128,128]{3,2,1,0:T(8,128)S(1)} fusion(f32[1,7,128,128]{3,2,1,0:T(8,128)S(1)} %bitcast.20, f32[1,7,128,128]{3,2,1,0:T(8,128)} %bitcast.21, f32[1,7,128,128]{3,2,1,0:T(8,128)} %bitcast.6, f32[1,7,128,128]{3,2,1,0:T(8,128)} %bitcast.5), kind=kLoop, calls=%fused_computation | loop fusion | flops 1376256 | bytes 3670016 | tf_op jit(solution)/shard_map/stack | solution.py:240
  77.3 2.7 %all-gather.4.cloned.1.call-done.lead = f32[16,128,128]{2,1,0:T(8,128)} async-done(((f32[1,128,128]{2,1,0:T(8,128)}), f32[16,128,128]{2,1,0:T(8,128)}) %all-gather.4.cloned.1.call-update) | async-done | bytes 1048592 | tf_op jit(solution)/shard_map/all_gather | solution.py:225
  80.0 0.0 copy-start.6
  80.0 1.2 copy-done.6
  81.3 22.0 %shard_map.47 = (f32[512,512]{1,0:T(8,128)S(1)}, f32[512,512]{1,0:T(8,128)S(1)}) custom-call(s32[3]{0:T(128)S(1)} %pad_add_fusion.scal, f32[16,128,128]{2,1,0:T(8,128)S(1)} %copy-done.6, f32[4,128]{1,0:T(4,128)S(1)} %bitcast.18), custom_call_target="tpu_custom_call" | custom-call | flops 20000000000 | bytes 4194304 | tf_op jit(solution)/shard_map/pallas_call | solution.py:242
  103.3 0.0 copy-start.1
  103.3 1.0 copy-done.1
  104.3 0.0 copy-start.3
  104.3 1.0 copy-done.3
  105.3 0.0 all-gather.6.cloned.1.call-done
  105.3 0.0 copy-start
  105.3 1.5 %copy-done = f32[28,128,128]{2,1,0:T(8,128)S(1)} copy-done((f32[28,128,128]{2,1,0:T(8,128)S(1)}, f32[28,128,128]{2,1,0:T(8,128)}, u32[]{:S(2)}) %copy-start) | copy-done | bytes 1835032
  106.8 0.0 copy-start.2
  106.8 1.2 copy-done.2
  108.0 0.0 copy-start.4
  108.0 1.2 copy-done.4
  109.2 24.3 %shard_map.48 = f32[8,1024,128]{2,1,0:T(8,128)} custom-call(s32[3]{0:T(128)S(1)} %pad_add_fusion.scal, s32[16]{0:T(128)S(1)} %reshape.16.targets, f32[16,128,128]{2,1,0:T(8,128)S(1)} %bitcast.15, f32[4,7,128,128]{3,2,1,0:T(8,128)S(1)} %bitcast.16, f32[4,7,128,128]{3,2,1,0:T(8,128)S(1)} %pad_maximum_fusion.col_part, f32[512,512]{1,0:T(8,128)S(1)} %copy-done.4, ...), custom_call_target="tpu_custom_call" | custom-call | tf_op jit(solution)/shard_map/pallas_call | solution.py:257
  (1 shorter events, 0.0 us)
Async XLA Ops:
  6.5 3.8 %copy-start.8 = (s32[1,1,1,2,8]{4,3,2,1,0:T(2,128)S(1)}, s32[1,1,1,2,8]{4,3,2,1,0:T(2,128)}, u32[]{:S(2)}) copy-start(s32[1,1,1,2,8]{4,3,2,1,0:T(2,128)} %param.5) | copy-start | bytes 196
  6.5 16.7 %all-to-all-start = ((f32[2,8,128,128]{3,2,1,0:T(8,128)}), f32[2,8,128,128]{3,2,1,0:T(8,128)S(1)}, u32[]{:S(2)}, u32[]{:S(2)}) async-start(f32[2,8,128,128]{3,2,1,0:T(8,128)} %bitcast.19), calls=%async_computation | async-start | bytes 2097152 | tf_op jit(solution)/shard_map/all_to_all | solution.py:213
  10.3 23.1 %copy-start.5 = (f32[1,4096]{1,0:T(1,128)S(1)}, f32[1,4096]{1,0:T(1,128)}, u32[]{:S(2)}) copy-start(f32[1,4096]{1,0:T(1,128)} %param.6) | copy-start | bytes 49156
  10.3 69.8 %all-gather.4.cloned.1.call-start = ((), (), s32[]{:S(2)}) async-start(), calls=%async_computation.1 | async-start | bytes 1114112 | tf_op jit(solution)/shard_map/all_gather | solution.py:225
  24.7 80.5 %all-gather.6.cloned.1.call-start = ((), (), s32[]{:S(2)}) async-start(), calls=%async_computation.2 | async-start | bytes 2293760 | tf_op jit(solution)/shard_map/all_gather | solution.py:239
  25.6 21.1 %collective-permute-start.3 = (f32[7,128,128]{2,1,0:T(8,128)}, f32[7,128,128]{2,1,0:T(8,128)S(1)}, u32[]{:S(2)}, u32[]{:S(2)}) collective-permute-start(f32[7,128,128]{2,1,0:T(8,128)} %slice.16), channel_id=1, source_target_pairs={{0,12},{1,0},{2,4},{3,8},{4,13},{5,1},{6,5},{7,9},{8,14},{9,2},{10... | collective-permute-start | bytes 1376264 | tf_op jit(solution)/shard_map/ppermute | solution.py:228
  28.1 46.9 %collective-permute-start.2 = (f32[7,128,128]{2,1,0:T(8,128)}, f32[7,128,128]{2,1,0:T(8,128)S(1)}, u32[]{:S(2)}, u32[]{:S(2)}) collective-permute-start(f32[7,128,128]{2,1,0:T(8,128)} %slice.16), channel_id=1, source_target_pairs={{0,8},{1,12},{2,0},{3,4},{4,9},{5,13},{6,1},{7,5},{8,10},{9,14},{1... | collective-permute-start | bytes 1376264 | tf_op jit(solution)/shard_map/ppermute | solution.py:228
  29.4 46.1 %collective-permute-start.1 = (f32[7,128,128]{2,1,0:T(8,128)}, f32[7,128,128]{2,1,0:T(8,128)}, u32[]{:S(2)}, u32[]{:S(2)}) collective-permute-start(f32[7,128,128]{2,1,0:T(8,128)} %slice.16), channel_id=1, source_target_pairs={{0,4},{1,8},{2,12},{3,0},{4,5},{5,9},{6,13},{7,1},{8,6},{9,10},{10... | collective-permute-start | bytes 1376264 | tf_op jit(solution)/shard_map/ppermute | solution.py:228
  30.2 45.3 %collective-permute-start = (f32[7,128,128]{2,1,0:T(8,128)}, f32[7,128,128]{2,1,0:T(8,128)}, u32[]{:S(2)}, u32[]{:S(2)}) collective-permute-start(f32[7,128,128]{2,1,0:T(8,128)} %slice.16), channel_id=1, source_target_pairs={{0,0},{1,4},{2,8},{3,12},{4,1},{5,5},{6,9},{7,13},{8,2},{9,6},{10,... | collective-permute-start | bytes 1376264 | tf_op jit(solution)/shard_map/ppermute | solution.py:228
  75.0 0.8 copy-start.7
  80.0 1.2 copy-start.6
  103.3 1.0 copy-start.1
  104.3 1.0 copy-start.3
  105.3 1.5 %copy-start = (f32[28,128,128]{2,1,0:T(8,128)S(1)}, f32[28,128,128]{2,1,0:T(8,128)}, u32[]{:S(2)}) copy-start(f32[28,128,128]{2,1,0:T(8,128)} %all-gather.6.cloned.1.call-done) | copy-start | bytes 5505028
  106.8 1.2 copy-start.2
  108.0 1.2 copy-start.4
Sparse Core Ops, SparseCore 0:
  24.9 55.1 all-gather.3
  81.6 20.2 all-gather.5

commit v2 on v1

--- a/solution.py
+++ b/solution.py
@@ -47,6 +47,55 @@
         return carry
 
     lax.fori_loop(0, slots, body, 0)
+
+
+def lead_kernel(rows_n, cols_n, src, out, got, send, recv):
+    r, c = lax.axis_index("row"), lax.axis_index("col")
+    sibling = c + 1 - 2 * lax.rem(c, 2)
+    mate = lax.rem(c + 2, cols_n)
+    others = [{"row": lax.rem(r + d, rows_n)} for d in range(1, rows_n)]
+    barrier = pltpu.get_barrier_semaphore()
+    for device in others + [{"col": sibling}, {"col": mate}]:
+        pl.semaphore_signal(barrier, inc=1, device_id=device, device_id_type=pl.DeviceIdType.MESH)
+    got[c, r] = src[...]
+    pl.semaphore_wait(barrier, rows_n + 1)
+
+    def copy(column, place, device, at):
+        block = got.at[column, place]
+        return pltpu.make_async_remote_copy(
+            src_ref=block,
+            dst_ref=block,
+            send_sem=send.at[at],
+            recv_sem=recv.at[at],
+            device_id=device,
+            device_id_type=pl.DeviceIdType.MESH,
+        )
+
+    down = [copy(c, r, device, d) for d, device in enumerate(others)]
+    for one in down:
+        one.start()
+    base = rows_n - 1
+    near, far, passed = [], [], []
+    for d in range(rows_n):
+        place = lax.rem(r - d + rows_n, rows_n)
+        if d:
+            down[d - 1].wait_recv()
+        far.append(copy(c, place, {"col": mate}, base + d))
+        near.append(copy(c, place, {"col": sibling}, base + rows_n + d))
+        far[-1].start()
+        near[-1].start()
+    for d in range(rows_n):
+        place = lax.rem(r - d + rows_n, rows_n)
+        far[d].wait_recv()
+        passed.append(copy(mate, place, {"col": sibling}, base + 2 * rows_n + d))
+        passed[-1].start()
+    for one in near + passed:
+        one.wait_recv()
+    for one in down + far + near + passed:
+        one.wait_send()
+    for j in range(cols_n):
+        for i in range(rows_n):
+            out[j * rows_n + i] = got[j, i]
 
 
 def invert_diagonal(block, bs):
@@ -95,7 +144,7 @@
     eye = row == col
     for i in range(NP):
         for j in range(i + 1):
-            block = lead[i * NP + j]
+            block = lead[j * NP + i]
             if i == j:
                 block = jnp.where(row >= col, block, block.T)
                 block = block + jnp.where(eye, stiff[i : i + 1, :], 0.0)
@@ -128,31 +177,30 @@
 
 def update_kernel(
     slots, across, rows_n, cols_n, bs, scal, targets, blocks, row_part, col_part, full, inverse,
-    stiff, out, inv_hi, inv_lo, col_hi, col_lo, total,
+    stiff, out, row_x, col_hi, col_lo, total,
 ):
     i = pl.program_id(0)
-    down = pl.num_programs(0)
+    down = row_part.shape[1] + 1
     r, c, pivot = scal[0], scal[1], scal[2]
 
-    def solved(part, k, place, owners):
-        def first():
-            return full[pl.ds(pl.multiple_of(place * bs, bs), bs), :]
-
-        a = jnp.concatenate([part[owner, jnp.maximum(k - 1, 0)] for owner in owners], axis=1)
-        a = jnp.where(k == 0, first(), a)
-        return split_dot(split(a), (inv_hi[...], inv_lo[...]), NT)
+    def solved(part, place, owners, inv):
+        first = full[pl.ds(pl.multiple_of(place * bs, bs), bs), :]
+        rest = jnp.concatenate(
+            [part[owner].reshape((down - 1) * bs, bs) for owner in owners], axis=1
+        )
+        return split_dot(split(jnp.concatenate([first, rest], axis=0)), inv, NT)
 
     @pl.when(i == 0)
     def _():
-        high, low = split(inverse[...])
-        inv_hi[...] = high
-        inv_lo[...] = low
-
-    high, low = split(solved(col_part, i, c, [lax.rem(r - j + rows_n, rows_n) for j in range(NP)]))
-    at = pl.ds(pl.multiple_of(i * bs, bs), bs)
-    col_hi[at, :] = high
-    col_lo[at, :] = low
-    x = solved(row_part, i, r, range(NP))
+        inv = split(inverse[...])
+        high, low = split(
+            solved(col_part, c, [lax.rem(r - j + rows_n, rows_n) for j in range(NP)], inv)
+        )
+        col_hi[...] = high
+        col_lo[...] = low
+        row_x[...] = solved(row_part, r, range(NP), inv)
+
+    x = row_x[pl.ds(pl.multiple_of(i * bs, bs), bs), :]
     mine = split(x)
     total[...] = jnp.zeros_like(total)
 
@@ -222,11 +270,24 @@
         out_specs=vmem,
         compiler_params=params,
     )(targets, blocks)
-    lead = lax.all_gather(panel[0], ("row", "col"), axis=0, tiled=False)
+    copies = 4 * rows_n - 1
+    lead = pl.pallas_call(
+        functools.partial(lead_kernel, rows_n, cols_n),
+        out_shape=jax.ShapeDtypeStruct((cols_n * rows_n, bs, bs), F32),
+        in_specs=[vmem],
+        out_specs=vmem,
+        scratch_shapes=[
+            pltpu.VMEM((cols_n, rows_n, bs, bs), F32),
+            pltpu.SemaphoreType.DMA((copies,)),
+            pltpu.SemaphoreType.DMA((copies,)),
+        ],
+        compiler_params=pltpu.CompilerParams(collective_id=0, has_side_effects=True),
+    )(panel[0])
     piece = panel[1:]
+    later, lead = lax.optimization_barrier((piece, lead))
     turned = [
         lax.ppermute(
-            piece,
+            piece if k < 2 else later,
             ("row", "col"),
             [
                 (a * cols_n + b, (b + k) % rows_n * cols_n + a)
@@ -270,8 +331,7 @@
         ],
         out_specs=pl.BlockSpec((1, bs * across, bs), lambda i: (i, 0, 0)),
         scratch_shapes=[
-            pltpu.VMEM((n, n), BF16),
-            pltpu.VMEM((n, n), BF16),
+            pltpu.VMEM((down * bs, n), F32),
             pltpu.VMEM((across * bs, n), BF16),
             pltpu.VMEM((across * bs, n), BF16),
             pltpu.VMEM((across, bs, bs), F32),

time: 142 us -> 138 us (0.972)
  waiting for transfers between devices: 57.7 us -> 19.3 us
  Pallas kernels: 47.2 us -> 82.4 us
    pallas_call x0 -> x1, Pallas kernels: none -> 40.5 us  [on_device(): pl.pallas_call(functools.partial(lead_kernel, rows_n, cols_n), out_shape=...]
    ppermute x4, waiting for transfers between devices: 42.1 us -> 6.45 us  [on_device(): lax.ppermute(piece if k < 2 else later, ('row', 'col'), [(a * cols_n + b,...]
    pallas_call x1, Pallas kernels: 24.3 us -> 19 us  [on_device(): pl.pallas_call(functools.partial(update_kernel, slots, across, rows_n, co...]
    all_gather x1 -> x0, waiting for transfers between devices: 2.75 us -> none  [on_device(): lead = lax.all_gather(panel[0], ('row', 'col'), axis=0, tiled=False)]
    unnamed x18 -> x20, local copies, waits for them, and re-layouts: 7.45 us -> 7.14 us
  transfers between devices with their start and end apart: 7 -> 6, of which waited for: 5 -> 2; matrix products, arithmetic and copies ran while one was open for 2% -> 2% of each run, Pallas kernels for 16% -> 46%
where the time goes in v2:
time: 138 us; the launch traced here: 137 us
  Pallas kernels  82.4 us (60%)
  waiting for transfers between devices  19.3 us (14%)
  between operations  14.2 us (10%)
  starting transfers between devices  11.3 us (8%)
  local copies, waits for them, and re-layouts  8.66 us (6%)
  other arithmetic  1.47 us (1%)
    pallas_call x1, Pallas kernels, on_device(): pl.pallas_call(functools.partial(lead_kernel, rows_n, cols_n), out_shape=...  40.5 us
    pallas_call x1, Pallas kernels, on_device(): pl.pallas_call(functools.partial(factor_kernel, bs), out_shape=[jax.Shape...  22 us
    pallas_call x1, Pallas kernels, on_device(): pl.pallas_call(functools.partial(update_kernel, slots, across, rows_n, co...  19 us
    all_to_all x1, waiting for transfers between devices, on_device(): lax.all_to_all(outgoing, 'front', split_axis=0, concat_axis=0, tiled=True)  12.8 us
    ppermute x4, starting transfers between devices, on_device(): lax.ppermute(piece if k < 2 else later, ('row', 'col'), [(a * cols_n + b,...  7.59 us
    unnamed x20, local copies, waits for them, and re-layouts  7.14 us
    ppermute x4, waiting for transfers between devices, on_device(): lax.ppermute(piece if k < 2 else later, ('row', 'col'), [(a * cols_n + b,...  6.45 us
    all_to_all x1, starting transfers between devices, on_device(): lax.all_to_all(outgoing, 'front', split_axis=0, concat_axis=0, tiled=True)  3.71 us
  transfers between devices with their start and end apart: 6, of which 2 were waited for; matrix products, arithmetic and copies ran while one was open for 2% of the time, Pallas kernels for 46%

profile of v2, /device:TPU:17, one launch (start us, length us, event | category | flops | bytes accessed | tf_op | source)
XLA Modules:
  0.0 137.4 jit_solution(12601899677039084552)
XLA Ops:
  6.5 0.0 copy-start.9
  6.5 3.7 %all-to-all-start = ((f32[2,8,128,128]{3,2,1,0:T(8,128)}), f32[2,8,128,128]{3,2,1,0:T(8,128)S(1)}, u32[]{:S(2)}, u32[]{:S(2)}) async-start(f32[2,8,128,128]{3,2,1,0:T(8,128)} %bitcast.21), calls=%async_computation | async-start | bytes 2097152 | tf_op jit(solution)/shard_map/all_to_all | solution.py:261
  10.3 0.0 copy-start.6
  10.3 0.0 all-gather.3.cloned.1.call-start
  10.3 0.0 copy-done.9
  10.3 0.1 reshape.16.targets
  10.4 12.8 %all-to-all-done = f32[2,8,128,128]{3,2,1,0:T(8,128)S(1)} async-done(((f32[2,8,128,128]{3,2,1,0:T(8,128)}), f32[2,8,128,128]{3,2,1,0:T(8,128)S(1)}, u32[]{:S(2)}, u32[]{:S(2)}) %all-to-all-start) | async-done | bytes 1048608 | tf_op jit(solution)/shard_map/all_to_all | solution.py:261
  23.2 0.8 shard_map.46
  24.1 0.8 slice.16
  24.9 0.0 all-gather.3.cloned.1.call-update
  25.6 0.0 copy-done.6
  25.6 0.1 pad_add_fusion.scal
  25.7 2.7 %collective-permute-start.1 = (f32[7,128,128]{2,1,0:T(8,128)}, f32[7,128,128]{2,1,0:T(8,128)S(1)}, u32[]{:S(2)}, u32[]{:S(2)}) collective-permute-start(f32[7,128,128]{2,1,0:T(8,128)} %slice.16), channel_id=1, source_target_pairs={{0,4},{1,8},{2,12},{3,0},{4,5},{5,9},{6,13},{7,1},{8,6},{9,10},{10... | collective-permute-start | bytes 1376264 | tf_op jit(solution)/shard_map/ppermute | solution.py:289
  28.4 2.9 %collective-permute-start = (f32[7,128,128]{2,1,0:T(8,128)}, f32[7,128,128]{2,1,0:T(8,128)S(1)}, u32[]{:S(2)}, u32[]{:S(2)}) collective-permute-start(f32[7,128,128]{2,1,0:T(8,128)} %slice.16), channel_id=1, source_target_pairs={{0,0},{1,4},{2,8},{3,12},{4,1},{5,5},{6,9},{7,13},{8,2},{9,6},{10,... | collective-permute-start | bytes 1376264 | tf_op jit(solution)/shard_map/ppermute | solution.py:289
  31.2 0.6 slice_bitcast_fusion.src
  31.9 40.5 %shard_map.47.lead = f32[16,128,128]{2,1,0:T(8,128)} custom-call(f32[128,128]{1,0:T(8,128)} %slice_bitcast_fusion.src), custom_call_target="tpu_custom_call" | custom-call | tf_op jit(solution)/shard_map/pallas_call | solution.py:274
  72.4 1.5 %collective-permute-start.3 = (f32[7,128,128]{2,1,0:T(8,128)}, f32[7,128,128]{2,1,0:T(8,128)S(1)}, u32[]{:S(2)}, u32[]{:S(2)}) collective-permute-start(f32[7,128,128]{2,1,0:T(8,128)} %slice.16), channel_id=1, source_target_pairs={{0,12},{1,0},{2,4},{3,8},{4,13},{5,1},{6,5},{7,9},{8,14},{9,2},{10... | collective-permute-start | bytes 1376264 | tf_op jit(solution)/shard_map/ppermute | solution.py:289
  74.0 0.5 collective-permute-start.2
  74.5 0.0 copy-start.1
  74.5 1.2 copy-done.1
  75.7 22.0 %shard_map.48 = (f32[512,512]{1,0:T(8,128)S(1)}, f32[512,512]{1,0:T(8,128)S(1)}) custom-call(s32[3]{0:T(128)S(1)} %pad_add_fusion.scal, f32[16,128,128]{2,1,0:T(8,128)S(1)} %copy-done.1, f32[4,128]{1,0:T(4,128)S(1)} %bitcast.20), custom_call_target="tpu_custom_call" | custom-call | flops 20000000000 | bytes 4194304 | tf_op jit(solution)/shard_map/pallas_call | solution.py:303
  97.7 0.0 copy-start.2
  97.7 1.0 copy-done.2
  98.7 0.0 copy-start.4
  98.7 1.0 copy-done.4
  99.7 0.0 collective-permute-done.1
  99.7 0.0 copy-start.7
  99.7 0.0 collective-permute-done
  99.7 0.0 copy-start.8
  99.7 0.0 collective-permute-done.3
  99.7 6.4 %collective-permute-done.2 = f32[7,128,128]{2,1,0:T(8,128)S(1)} collective-permute-done((f32[7,128,128]{2,1,0:T(8,128)}, f32[7,128,128]{2,1,0:T(8,128)S(1)}, u32[]{:S(2)}, u32[]{:S(2)}) %collective-permute-start.2) | collective-permute-done | bytes 458784 | tf_op jit(solution)/shard_map/ppermute | solution.py:289
  106.2 0.0 copy-done.7
  106.2 0.0 copy-done.8
  106.2 1.4 %pad_maximum_fusion.col_part = f32[4,7,128,128]{3,2,1,0:T(8,128)S(1)} fusion(f32[1,7,128,128]{3,2,1,0:T(8,128)S(1)} %bitcast.24, f32[1,7,128,128]{3,2,1,0:T(8,128)S(1)} %bitcast.25, f32[1,7,128,128]{3,2,1,0:T(8,128)} %bitcast.22, f32[1,7,128,128]{3,2,1,0:T(8,128)} %bitcast.23), kind=kLoop, calls=%fused_computation | loop fusion | flops 1376256 | bytes 3670016 | tf_op jit(solution)/shard_map/stack | solution.py:301
  107.6 0.0 all-gather.3.cloned.1.call-done
  107.6 0.0 copy-start
  107.6 1.5 %copy-done = f32[28,128,128]{2,1,0:T(8,128)S(1)} copy-done((f32[28,128,128]{2,1,0:T(8,128)S(1)}, f32[28,128,128]{2,1,0:T(8,128)}, u32[]{:S(2)}) %copy-start) | copy-done | bytes 1835032
  109.1 0.0 copy-start.3
  109.1 1.2 copy-done.3
  110.3 0.0 copy-start.5
  110.3 1.2 copy-done.5
  111.5 19.0 %shard_map.49 = f32[8,1024,128]{2,1,0:T(8,128)} custom-call(s32[3]{0:T(128)S(1)} %pad_add_fusion.scal, s32[16]{0:T(128)S(1)} %reshape.16.targets, f32[16,128,128]{2,1,0:T(8,128)S(1)} %bitcast.17, f32[4,7,128,128]{3,2,1,0:T(8,128)S(1)} %bitcast.18, f32[4,7,128,128]{3,2,1,0:T(8,128)S(1)} %pad_maximum_fusion.col_part, f32[512,512]{1,0:T(8,128)S(1)} %copy-done.5, ...), custom_call_target="tpu_custom_call" | custom-call | tf_op jit(solution)/shard_map/pallas_call | solution.py:318
  (1 shorter events, 0.0 us)
Async XLA Ops:
  6.5 3.8 %copy-start.9 = (s32[1,1,1,2,8]{4,3,2,1,0:T(2,128)S(1)}, s32[1,1,1,2,8]{4,3,2,1,0:T(2,128)}, u32[]{:S(2)}) copy-start(s32[1,1,1,2,8]{4,3,2,1,0:T(2,128)} %param.5) | copy-start | bytes 196
  6.5 16.7 %all-to-all-start = ((f32[2,8,128,128]{3,2,1,0:T(8,128)}), f32[2,8,128,128]{3,2,1,0:T(8,128)S(1)}, u32[]{:S(2)}, u32[]{:S(2)}) async-start(f32[2,8,128,128]{3,2,1,0:T(8,128)} %bitcast.21), calls=%async_computation | async-start | bytes 2097152 | tf_op jit(solution)/shard_map/all_to_all | solution.py:261
  10.3 15.3 %copy-start.6 = (f32[1,4096]{1,0:T(1,128)S(1)}, f32[1,4096]{1,0:T(1,128)}, u32[]{:S(2)}) copy-start(f32[1,4096]{1,0:T(1,128)} %param.6) | copy-start | bytes 49156
  10.3 97.3 %all-gather.3.cloned.1.call-start = ((), (), s32[]{:S(2)}) async-start(), calls=%async_computation.1 | async-start | bytes 2293760 | tf_op jit(solution)/shard_map/all_gather | solution.py:300
  25.7 74.0 %collective-permute-start.1 = (f32[7,128,128]{2,1,0:T(8,128)}, f32[7,128,128]{2,1,0:T(8,128)S(1)}, u32[]{:S(2)}, u32[]{:S(2)}) collective-permute-start(f32[7,128,128]{2,1,0:T(8,128)} %slice.16), channel_id=1, source_target_pairs={{0,4},{1,8},{2,12},{3,0},{4,5},{5,9},{6,13},{7,1},{8,6},{9,10},{10... | collective-permute-start | bytes 1376264 | tf_op jit(solution)/shard_map/ppermute | solution.py:289
  28.4 71.3 %collective-permute-start = (f32[7,128,128]{2,1,0:T(8,128)}, f32[7,128,128]{2,1,0:T(8,128)S(1)}, u32[]{:S(2)}, u32[]{:S(2)}) collective-permute-start(f32[7,128,128]{2,1,0:T(8,128)} %slice.16), channel_id=1, source_target_pairs={{0,0},{1,4},{2,8},{3,12},{4,1},{5,5},{6,9},{7,13},{8,2},{9,6},{10,... | collective-permute-start | bytes 1376264 | tf_op jit(solution)/shard_map/ppermute | solution.py:289
  72.4 27.3 %collective-permute-start.3 = (f32[7,128,128]{2,1,0:T(8,128)}, f32[7,128,128]{2,1,0:T(8,128)S(1)}, u32[]{:S(2)}, u32[]{:S(2)}) collective-permute-start(f32[7,128,128]{2,1,0:T(8,128)} %slice.16), channel_id=1, source_target_pairs={{0,12},{1,0},{2,4},{3,8},{4,13},{5,1},{6,5},{7,9},{8,14},{9,2},{10... | collective-permute-start | bytes 1376264 | tf_op jit(solution)/shard_map/ppermute | solution.py:289
  74.0 32.2 %collective-permute-start.2 = (f32[7,128,128]{2,1,0:T(8,128)}, f32[7,128,128]{2,1,0:T(8,128)S(1)}, u32[]{:S(2)}, u32[]{:S(2)}) collective-permute-start(f32[7,128,128]{2,1,0:T(8,128)} %slice.16), channel_id=1, source_target_pairs={{0,8},{1,12},{2,0},{3,4},{4,9},{5,13},{6,1},{7,5},{8,10},{9,14},{1... | collective-permute-start | bytes 1376264 | tf_op jit(solution)/shard_map/ppermute | solution.py:289
  74.5 1.2 copy-start.1
  97.7 1.0 copy-start.2
  98.7 1.0 copy-start.4
  99.7 6.5 %copy-start.7 = (f32[7,128,128]{2,1,0:T(8,128)}, f32[7,128,128]{2,1,0:T(8,128)S(1)}, u32[]{:S(2)}) copy-start(f32[7,128,128]{2,1,0:T(8,128)S(1)} %collective-permute-done.1) | copy-start | bytes 1376260
  99.7 6.5 %copy-start.8 = (f32[7,128,128]{2,1,0:T(8,128)}, f32[7,128,128]{2,1,0:T(8,128)S(1)}, u32[]{:S(2)}) copy-start(f32[7,128,128]{2,1,0:T(8,128)S(1)} %collective-permute-done) | copy-start | bytes 1376260
  107.6 1.5 %copy-start = (f32[28,128,128]{2,1,0:T(8,128)S(1)}, f32[28,128,128]{2,1,0:T(8,128)}, u32[]{:S(2)}) copy-start(f32[28,128,128]{2,1,0:T(8,128)} %all-gather.3.cloned.1.call-done) | copy-start | bytes 5505028
  109.1 1.2 copy-start.3
  110.3 1.2 copy-start.5
Sparse Core Ops, SparseCore 0:
  25.0 28.8 all-gather.2

commit v3 on v2

--- a/solution.py
+++ b/solution.py
@@ -176,29 +176,29 @@
 
 
 def update_kernel(
-    slots, across, rows_n, cols_n, bs, scal, targets, blocks, row_part, col_part, full, inverse,
-    stiff, out, row_x, col_hi, col_lo, total,
+    slots, across, rows_n, cols_n, bs, scal, targets, blocks, row_part, col_0, col_1, col_2, col_3,
+    full, inverse, stiff, out, row_x, col_hi, col_lo, total,
 ):
     i = pl.program_id(0)
     down = row_part.shape[1] + 1
     r, c, pivot = scal[0], scal[1], scal[2]
 
-    def solved(part, place, owners, inv):
-        first = full[pl.ds(pl.multiple_of(place * bs, bs), bs), :]
-        rest = jnp.concatenate(
-            [part[owner].reshape((down - 1) * bs, bs) for owner in owners], axis=1
-        )
-        return split_dot(split(jnp.concatenate([first, rest], axis=0)), inv, NT)
-
     @pl.when(i == 0)
     def _():
         inv = split(inverse[...])
-        high, low = split(
-            solved(col_part, c, [lax.rem(r - j + rows_n, rows_n) for j in range(NP)], inv)
-        )
+        row_x[0:bs, :] = full[pl.ds(pl.multiple_of(c * bs, bs), bs), :]
+        for k, part in enumerate((col_0, col_1, col_2, col_3)):
+            owner = lax.rem(r - k + rows_n, rows_n)
+            at = pl.ds(pl.multiple_of(owner * bs, bs), bs)
+            row_x[bs : down * bs, at] = part[...].reshape((down - 1) * bs, bs)
+        high, low = split(split_dot(split(row_x[...]), inv, NT))
         col_hi[...] = high
         col_lo[...] = low
-        row_x[...] = solved(row_part, r, range(NP), inv)
+        first = full[pl.ds(pl.multiple_of(r * bs, bs), bs), :]
+        rest = jnp.concatenate(
+            [row_part[j].reshape((down - 1) * bs, bs) for j in range(NP)], axis=1
+        )
+        row_x[...] = split_dot(split(jnp.concatenate([first, rest], axis=0)), inv, NT)
 
     x = row_x[pl.ds(pl.multiple_of(i * bs, bs), bs), :]
     mine = split(x)
@@ -284,10 +284,10 @@
         compiler_params=pltpu.CompilerParams(collective_id=0, has_side_effects=True),
     )(panel[0])
     piece = panel[1:]
-    later, lead = lax.optimization_barrier((piece, lead))
+    piece, lead = lax.optimization_barrier((piece, lead))
     turned = [
         lax.ppermute(
-            piece if k < 2 else later,
+            piece,
             ("row", "col"),
             [
                 (a * cols_n + b, (b + k) % rows_n * cols_n + a)
@@ -298,7 +298,6 @@
         for k in range(NP)
     ]
     row_part = lax.all_gather(piece, "col", axis=0, tiled=False)
-    col_part = jnp.stack(turned)
     n = NP * bs
     inverse, full = pl.pallas_call(
         functools.partial(factor_kernel, bs),
@@ -324,7 +323,7 @@
             smem,
             whole(blocks.shape),
             whole(row_part.shape),
-            whole(col_part.shape),
+            *[whole(piece.shape)] * NP,
             whole((n, n)),
             whole((n, n)),
             whole(stiff.shape),
@@ -337,7 +336,7 @@
             pltpu.VMEM((across, bs, bs), F32),
         ],
         compiler_params=params,
-    )(scal, targets, blocks, row_part, col_part, full, inverse, stiff)
+    )(scal, targets, blocks, row_part, *turned, full, inverse, stiff)
     return result.reshape(1, 1, down, bs, 1, across, bs)
 
 

time: 138 us -> 122 us (0.88)
  Pallas kernels: 82.4 us -> 58.6 us
  waiting for transfers between devices: 19.3 us -> 25.4 us
  local copies, waits for them, and re-layouts: 8.66 us -> 12.3 us
  other arithmetic: 1.47 us -> 0.08 us
    pallas_call x1, Pallas kernels: 40.5 us -> 16.3 us  [on_device(): pl.pallas_call(functools.partial(lead_kernel, rows_n, cols_n), out_shape=...]
    ppermute x4, waiting for transfers between devices: 6.45 us -> 13.2 us  [on_device(): lax.ppermute(piece, ('row', 'col'), [(a * cols_n + b, (b + k) % rows_n *...]
    unnamed x20 -> x22, local copies, waits for them, and re-layouts: 7.14 us -> 10.1 us
    another operation x1 -> x0, other arithmetic: 1.39 us -> none  [on_device(): col_part = jnp.stack(turned)]
  transfers between devices with their start and end apart: 6 -> 6, of which waited for: 2 -> 2; matrix products, arithmetic and copies ran while one was open for 2% -> 1% of each run, Pallas kernels for 46% -> 18%
where the time goes in v3:
time: 122 us; the launch traced here: 121 us
  Pallas kernels  58.6 us (48%)
  waiting for transfers between devices  25.4 us (21%)
  between operations  14.1 us (12%)
  local copies, waits for them, and re-layouts  12.3 us (10%)
  starting transfers between devices  10.7 us (9%)
    pallas_call x1, Pallas kernels, on_device(): pl.pallas_call(functools.partial(factor_kernel, bs), out_shape=[jax.Shape...  22 us
    pallas_call x1, Pallas kernels, on_device(): pl.pallas_call(functools.partial(update_kernel, slots, across, rows_n, co...  19.3 us
    pallas_call x1, Pallas kernels, on_device(): pl.pallas_call(functools.partial(lead_kernel, rows_n, cols_n), out_shape=...  16.3 us
    ppermute x4, waiting for transfers between devices, on_device(): lax.ppermute(piece, ('row', 'col'), [(a * cols_n + b, (b + k) % rows_n *...  13.2 us
    all_to_all x1, waiting for transfers between devices, on_device(): lax.all_to_all(outgoing, 'front', split_axis=0, concat_axis=0, tiled=True)  12.2 us
    unnamed x22, local copies, waits for them, and re-layouts  10.1 us
    ppermute x4, starting transfers between devices, on_device(): lax.ppermute(piece, ('row', 'col'), [(a * cols_n + b, (b + k) % rows_n *...  6.91 us
    all_to_all x1, starting transfers between devices, on_device(): lax.all_to_all(outgoing, 'front', split_axis=0, concat_axis=0, tiled=True)  3.71 us
  transfers between devices with their start and end apart: 6, of which 2 were waited for; matrix products, arithmetic and copies ran while one was open for 1% of the time, Pallas kernels for 18%

profile of v3, /device:TPU:17, one launch (start us, length us, event | category | flops | bytes accessed | tf_op | source)
XLA Modules:
  0.0 121.1 jit_solution(17054958831730559174)
XLA Ops:
  6.5 0.0 copy-start.10
  6.5 3.7 %all-to-all-start = ((f32[2,8,128,128]{3,2,1,0:T(8,128)}), f32[2,8,128,128]{3,2,1,0:T(8,128)S(1)}, u32[]{:S(2)}, u32[]{:S(2)}) async-start(f32[2,8,128,128]{3,2,1,0:T(8,128)} %bitcast.17), calls=%async_computation | async-start | bytes 2097152 | tf_op jit(solution)/shard_map/all_to_all | solution.py:261
  10.3 0.0 all-gather.3.cloned.1.call-start
  10.3 0.8 reshape.16.targets
  11.1 12.2 %all-to-all-done = f32[2,8,128,128]{3,2,1,0:T(8,128)S(1)} async-done(((f32[2,8,128,128]{3,2,1,0:T(8,128)}), f32[2,8,128,128]{3,2,1,0:T(8,128)S(1)}, u32[]{:S(2)}, u32[]{:S(2)}) %all-to-all-start) | async-done | bytes 1048608 | tf_op jit(solution)/shard_map/all_to_all | solution.py:261
  23.2 0.9 shard_map.46
  24.1 0.6 slice_bitcast_fusion.src
  24.7 0.8 slice.16
  25.5 16.3 %shard_map.47.lead = f32[16,128,128]{2,1,0:T(8,128)} custom-call(f32[128,128]{1,0:T(8,128)} %slice_bitcast_fusion.src), custom_call_target="tpu_custom_call" | custom-call | tf_op jit(solution)/shard_map/pallas_call | solution.py:274
  41.9 0.0 all-gather.3.cloned.1.call-update
  42.6 0.0 copy-done.10
  42.6 0.1 pad_add_fusion.scal
  42.7 1.5 %collective-permute-start.3 = (f32[7,128,128]{2,1,0:T(8,128)}, f32[7,128,128]{2,1,0:T(8,128)S(1)}, u32[]{:S(2)}, u32[]{:S(2)}) collective-permute-start(f32[7,128,128]{2,1,0:T(8,128)} %slice.16), channel_id=1, source_target_pairs={{0,12},{1,0},{2,4},{3,8},{4,13},{5,1},{6,5},{7,9},{8,14},{9,2},{10... | collective-permute-start | bytes 1376264 | tf_op jit(solution)/shard_map/ppermute | solution.py:289
  44.1 0.7 collective-permute-start.2
  44.8 1.4 %collective-permute-start.1 = (f32[7,128,128]{2,1,0:T(8,128)}, f32[7,128,128]{2,1,0:T(8,128)S(1)}, u32[]{:S(2)}, u32[]{:S(2)}) collective-permute-start(f32[7,128,128]{2,1,0:T(8,128)} %slice.16), channel_id=1, source_target_pairs={{0,4},{1,8},{2,12},{3,0},{4,5},{5,9},{6,13},{7,1},{8,6},{9,10},{10... | collective-permute-start | bytes 1376264 | tf_op jit(solution)/shard_map/ppermute | solution.py:289
  46.2 3.3 %collective-permute-start = (f32[7,128,128]{2,1,0:T(8,128)}, f32[7,128,128]{2,1,0:T(8,128)S(1)}, u32[]{:S(2)}, u32[]{:S(2)}) collective-permute-start(f32[7,128,128]{2,1,0:T(8,128)} %slice.16), channel_id=1, source_target_pairs={{0,0},{1,4},{2,8},{3,12},{4,1},{5,5},{6,9},{7,13},{8,2},{9,6},{10,... | collective-permute-start | bytes 1376264 | tf_op jit(solution)/shard_map/ppermute | solution.py:289
  49.6 0.0 copy-start.1
  49.6 1.4 %copy-done.1 = f32[16,128,128]{2,1,0:T(8,128)S(1)} copy-done((f32[16,128,128]{2,1,0:T(8,128)S(1)}, f32[16,128,128]{2,1,0:T(8,128)}, u32[]{:S(2)}) %copy-start.1) | copy-done | bytes 1048600
  51.0 22.0 %shard_map.48 = (f32[512,512]{1,0:T(8,128)S(1)}, f32[512,512]{1,0:T(8,128)S(1)}) custom-call(s32[3]{0:T(128)S(1)} %pad_add_fusion.scal, f32[16,128,128]{2,1,0:T(8,128)S(1)} %copy-done.1, f32[4,128]{1,0:T(4,128)S(1)} %bitcast.16), custom_call_target="tpu_custom_call" | custom-call | flops 20000000000 | bytes 4194304 | tf_op jit(solution)/shard_map/pallas_call | solution.py:302
  73.1 0.0 collective-permute-done.3.col_3
  73.1 0.0 copy-start.2
  73.1 0.8 copy-done.2
  73.8 13.2 %collective-permute-done.2.col_2 = f32[7,128,128]{2,1,0:T(8,128)S(1)} collective-permute-done((f32[7,128,128]{2,1,0:T(8,128)}, f32[7,128,128]{2,1,0:T(8,128)S(1)}, u32[]{:S(2)}, u32[]{:S(2)}) %collective-permute-start.2) | collective-permute-done | bytes 458784 | tf_op jit(solution)/shard_map/ppermute | solution.py:289
  87.0 0.0 copy-start.4
  87.0 0.8 copy-done.4
  87.8 0.0 collective-permute-done.1.col_1
  87.8 0.0 copy-start.6
  87.8 0.8 copy-done.6
  88.6 0.0 collective-permute-done.col_0
  88.6 0.0 copy-start.8
  88.6 0.8 copy-done.8
  89.4 0.0 all-gather.3.cloned.1.call-done
  89.4 0.0 copy-start
  89.4 1.5 %copy-done = f32[28,128,128]{2,1,0:T(8,128)S(1)} copy-done((f32[28,128,128]{2,1,0:T(8,128)S(1)}, f32[28,128,128]{2,1,0:T(8,128)}, u32[]{:S(2)}) %copy-start) | copy-done | bytes 1835032
  90.9 0.0 copy-start.3
  90.9 1.0 copy-done.3
  91.9 0.0 copy-start.5
  91.9 1.0 copy-done.5
  92.9 0.0 copy-start.7
  92.9 1.0 copy-done.7
  93.9 0.0 copy-start.9
  93.9 1.0 copy-done.9
  95.0 19.3 %shard_map.49 = f32[8,1024,128]{2,1,0:T(8,128)} custom-call(s32[3]{0:T(128)S(1)} %pad_add_fusion.scal, s32[16]{0:T(128)S(1)} %reshape.16.targets, f32[16,128,128]{2,1,0:T(8,128)S(1)} %bitcast.13, f32[4,7,128,128]{3,2,1,0:T(8,128)S(1)} %bitcast.14, f32[7,128,128]{2,1,0:T(8,128)S(1)} %copy-done.9, f32[7,128,128]{2,1,0:T(8,128)S(1)} %copy-done.7, ...), custom_call_target="tpu_custom_call" | custom-call | tf_op jit(solution)/shard_map/pallas_call | solution.py:317
  (1 shorter events, 0.0 us)
Async XLA Ops:
  6.5 36.0 %copy-start.10 = (f32[1,4096]{1,0:T(1,128)S(1)}, f32[1,4096]{1,0:T(1,128)}, u32[]{:S(2)}) copy-start(f32[1,4096]{1,0:T(1,128)} %param.6) | copy-start | bytes 49156
  6.5 16.7 %all-to-all-start = ((f32[2,8,128,128]{3,2,1,0:T(8,128)}), f32[2,8,128,128]{3,2,1,0:T(8,128)S(1)}, u32[]{:S(2)}, u32[]{:S(2)}) async-start(f32[2,8,128,128]{3,2,1,0:T(8,128)} %bitcast.17), calls=%async_computation | async-start | bytes 2097152 | tf_op jit(solution)/shard_map/all_to_all | solution.py:261
  10.3 79.1 %all-gather.3.cloned.1.call-start = ((), (), s32[]{:S(2)}) async-start(), calls=%async_computation.1 | async-start | bytes 2293760 | tf_op jit(solution)/shard_map/all_gather | solution.py:300
  42.7 30.4 %collective-permute-start.3 = (f32[7,128,128]{2,1,0:T(8,128)}, f32[7,128,128]{2,1,0:T(8,128)S(1)}, u32[]{:S(2)}, u32[]{:S(2)}) collective-permute-start(f32[7,128,128]{2,1,0:T(8,128)} %slice.16), channel_id=1, source_target_pairs={{0,12},{1,0},{2,4},{3,8},{4,13},{5,1},{6,5},{7,9},{8,14},{9,2},{10... | collective-permute-start | bytes 1376264 | tf_op jit(solution)/shard_map/ppermute | solution.py:289
  44.1 42.9 %collective-permute-start.2 = (f32[7,128,128]{2,1,0:T(8,128)}, f32[7,128,128]{2,1,0:T(8,128)S(1)}, u32[]{:S(2)}, u32[]{:S(2)}) collective-permute-start(f32[7,128,128]{2,1,0:T(8,128)} %slice.16), channel_id=1, source_target_pairs={{0,8},{1,12},{2,0},{3,4},{4,9},{5,13},{6,1},{7,5},{8,10},{9,14},{1... | collective-permute-start | bytes 1376264 | tf_op jit(solution)/shard_map/ppermute | solution.py:289
  44.8 43.0 %collective-permute-start.1 = (f32[7,128,128]{2,1,0:T(8,128)}, f32[7,128,128]{2,1,0:T(8,128)S(1)}, u32[]{:S(2)}, u32[]{:S(2)}) collective-permute-start(f32[7,128,128]{2,1,0:T(8,128)} %slice.16), channel_id=1, source_target_pairs={{0,4},{1,8},{2,12},{3,0},{4,5},{5,9},{6,13},{7,1},{8,6},{9,10},{10... | collective-permute-start | bytes 1376264 | tf_op jit(solution)/shard_map/ppermute | solution.py:289
  46.2 42.4 %collective-permute-start = (f32[7,128,128]{2,1,0:T(8,128)}, f32[7,128,128]{2,1,0:T(8,128)S(1)}, u32[]{:S(2)}, u32[]{:S(2)}) collective-permute-start(f32[7,128,128]{2,1,0:T(8,128)} %slice.16), channel_id=1, source_target_pairs={{0,0},{1,4},{2,8},{3,12},{4,1},{5,5},{6,9},{7,13},{8,2},{9,6},{10,... | collective-permute-start | bytes 1376264 | tf_op jit(solution)/shard_map/ppermute | solution.py:289
  49.6 1.4 %copy-start.1 = (f32[16,128,128]{2,1,0:T(8,128)S(1)}, f32[16,128,128]{2,1,0:T(8,128)}, u32[]{:S(2)}) copy-start(f32[16,128,128]{2,1,0:T(8,128)} %shard_map.47.lead) | copy-start | bytes 3145732
  73.1 0.8 copy-start.2
  87.0 0.8 copy-start.4
  87.8 0.8 copy-start.6
  88.6 0.8 copy-start.8
  89.4 1.5 %copy-start = (f32[28,128,128]{2,1,0:T(8,128)S(1)}, f32[28,128,128]{2,1,0:T(8,128)}, u32[]{:S(2)}) copy-start(f32[28,128,128]{2,1,0:T(8,128)} %all-gather.3.cloned.1.call-done) | copy-start | bytes 5505028
  90.9 1.0 copy-start.3
  91.9 1.0 copy-start.5
  92.9 1.0 copy-start.7
  93.9 1.0 copy-start.9
Sparse Core Ops, SparseCore 0:
  42.0 33.5 all-gather.2
